TPU v7x, 32 devices: a whole 2x2x4 slice. The times are simulated.
32 devices in a mesh: fsdp: 32 (over z, y, x, core).
Axes of the slice: x: 2, y: 2, z: 4, core: 2. Of those that a mesh axis runs over, the one named last changes fastest.
Arguments:
- tokens: bfloat16 [32768, 768], P('fsdp'), may hold values from -6 to 6
- cotangent: bfloat16 [32768, 768], P('fsdp'), may hold values from -6 to 6
- lengths: int32 [64, 3], P('fsdp'), may hold values from 1 to 384, 512 in all within a row
- w_qkv: float32 [768, 2304], P('fsdp'), may hold values from -0.21875 to 0.21875
- w_out: float32 [768, 768], P('fsdp'), may hold values from -1.25 to 1.25
- w_fc: float32 [768, 3072], P('fsdp'), may hold values from -0.21875 to 0.21875
- w_proj: float32 [3072, 768], P('fsdp'), may hold values from -0.109375 to 0.109375
- vectors: float32 [9216], P('fsdp'), may hold values from -0.6 to 3.5
- m_qkv: float32 [768, 2304], P('fsdp'), may hold values from -0.00016527923 to 0.00016527923
- m_out: float32 [768, 768], P('fsdp'), may hold values from -0.00016527923 to 0.00016527923
- m_fc: float32 [768, 3072], P('fsdp'), may hold values from -0.00016527923 to 0.00016527923
- m_proj: float32 [3072, 768], P('fsdp'), may hold values from -0.00016527923 to 0.00016527923
- m_vectors: float32 [9216], P('fsdp'), may hold values from -0.00016527923 to 0.00016527923
- s_qkv: float32 [768, 2304], P('fsdp'), may hold values from 1.4110135e-10 to 5.644054e-10
- s_out: float32 [768, 768], P('fsdp'), may hold values from 1.4110135e-10 to 5.644054e-10
- s_fc: float32 [768, 3072], P('fsdp'), may hold values from 1.4110135e-10 to 5.644054e-10
- s_proj: float32 [3072, 768], P('fsdp'), may hold values from 1.4110135e-10 to 5.644054e-10
- s_vectors: float32 [9216], P('fsdp'), may hold values from 1.4110135e-10 to 5.644054e-10
Outputs:
- output: bfloat16 [32768, 768], P('fsdp')
- input_grad: float32 [32768, 768], P('fsdp')
- grad_norm: float32 [], replicated
- new_qkv: float32 [768, 2304], P('fsdp')
- new_out: float32 [768, 768], P('fsdp')
- new_fc: float32 [768, 3072], P('fsdp')
- new_proj: float32 [3072, 768], P('fsdp')
- new_vectors: float32 [9216], P('fsdp')
- first_qkv: float32 [768, 2304], P('fsdp')
- first_out: float32 [768, 768], P('fsdp')
- first_fc: float32 [768, 3072], P('fsdp')
- first_proj: float32 [3072, 768], P('fsdp')
- first_vectors: float32 [9216], P('fsdp')
- second_qkv: float32 [768, 2304], P('fsdp')
- second_out: float32 [768, 768], P('fsdp')
- second_fc: float32 [768, 3072], P('fsdp')
- second_proj: float32 [3072, 768], P('fsdp')
- second_vectors: float32 [9216], P('fsdp')
Inputs may be any that keep to these rules, and one draw needn't show every extreme that they name: Each row's 3 lengths sum to 512, and the largest of each row is 384.
All inputs are finite; a program needn't handle non-finite values.
Results may differ from a plain program's by a relative error of at most 0.0095.
The roundings to bfloat16 on the way count: a program that leaves them out, or rounds other values in their place, can miss the bound.
Values may be sent and summed in bfloat16 or wider, within the bound.
A program may use at most 192 MiB of HBM per device.

v0:
```python
import jax
import jax.numpy as jnp
from jax import lax
from jax.sharding import PartitionSpec as P

D = 768
H = 12
HD = 64
STEP = 10


EPS_NORM = 1e-05
THRESH = 1.0
BETA_ONE = 0.9
BETA_TWO = 0.999
LR_MAT = 0.03
LR_VEC = 0.5
WEIGHT_DECAY = 0.1
EPS_ADAM = 1e-08
BIG_NEG = -1e30


def segment_ids(lengths_row, extent):
    ends_all = jnp.cumsum(lengths_row)
    places = jnp.arange(extent, dtype=jnp.int32)
    return jnp.sum((places[:, None] >= ends_all[None, :]).astype(jnp.int32), axis=1)


def norm_rows(values_in, scaling, offset):
    center = values_in - jnp.mean(values_in, axis=-1, keepdims=True)
    variance = jnp.mean(center * center, axis=-1, keepdims=True)
    return center * lax.rsqrt(variance + EPS_NORM) * scaling + offset


def split_vectors(vec_all):
    pieces = [vec_all[position * D : (position + 1) * D] for position in range(8)]
    return pieces + [vec_all[8 * D :]]


def gelu_tanh(z):
    return jax.nn.gelu(z, approximate=True)


def block_mask(segment, start, block_rows, columns):
    rows_here = start + jnp.arange(block_rows, dtype=jnp.int32)
    return (segment[:, None] == segment[None, :]) & (rows_here[:, None] >= columns[None, :])


def attend_forward(queries, keys_all, values_all, segment):
    extent = queries.shape[0]
    block_rows = min(extent, 512)
    block_count = extent // block_rows
    score_scale = HD ** (-0.5)
    query_blocks = queries.reshape(block_count, block_rows, H, HD)
    starts = jnp.arange(block_count, dtype=jnp.int32) * block_rows
    columns = jnp.arange(extent, dtype=jnp.int32)

    def one_block(payload):
        query_rows, start = payload
        allowed = block_mask(segment, start, block_rows, columns)
        scores = (
            jnp.einsum("qhd,khd->hqk", query_rows, keys_all, preferred_element_type=jnp.float32)
            * score_scale
        )
        scores = jnp.where(allowed[None], scores, BIG_NEG)
        highest = jnp.max(scores, axis=-1, keepdims=True)
        exponent = jnp.exp(scores - highest)
        totals = jnp.sum(exponent, axis=-1, keepdims=True)
        soft_probs = (exponent / totals).astype(jnp.bfloat16)
        attended = jnp.einsum(
            "hqk,khd->qhd", soft_probs, values_all, preferred_element_type=jnp.float32
        )
        return (attended, highest + jnp.log(totals))

    attended, log_totals = lax.map(one_block, (query_blocks, starts))
    return (attended.reshape(extent, D), log_totals)


def attend_backward(queries, keys_all, values_all, grad_att, log_totals, segment):
    extent = queries.shape[0]
    block_rows = min(extent, 512)
    block_count = extent // block_rows
    score_scale = HD ** (-0.5)
    query_blocks = queries.reshape(block_count, block_rows, H, HD)
    grad_blocks = grad_att.reshape(block_count, block_rows, H, HD)
    starts = jnp.arange(block_count, dtype=jnp.int32) * block_rows
    columns = jnp.arange(extent, dtype=jnp.int32)

    def one_block(carried, payload):
        grad_keys, grad_values = carried
        query_rows, grad_rows, log_rows, start = payload
        allowed = block_mask(segment, start, block_rows, columns)
        scores = (
            jnp.einsum("qhd,khd->hqk", query_rows, keys_all, preferred_element_type=jnp.float32)
            * score_scale
        )
        scores = jnp.where(allowed[None], scores, BIG_NEG)
        soft_probs = jnp.where(allowed[None], jnp.exp(scores - log_rows), 0.0)
        grad_values = grad_values + jnp.einsum(
            "hqk,qhd->khd",
            soft_probs.astype(jnp.bfloat16),
            grad_rows,
            preferred_element_type=jnp.float32,
        )
        grad_probs = jnp.einsum(
            "qhd,khd->hqk", grad_rows, values_all, preferred_element_type=jnp.float32
        )
        grad_scores = soft_probs * (
            grad_probs - jnp.sum(soft_probs * grad_probs, axis=-1, keepdims=True)
        )
        grad_scores = grad_scores.astype(jnp.bfloat16)
        grad_query = (
            jnp.einsum("hqk,khd->qhd", grad_scores, keys_all, preferred_element_type=jnp.float32)
            * score_scale
        )
        grad_keys = (
            grad_keys
            + jnp.einsum(
                "hqk,qhd->khd", grad_scores, query_rows, preferred_element_type=jnp.float32
            )
            * score_scale
        )
        return ((grad_keys, grad_values), grad_query)

    zero_heads = jnp.zeros((extent, H, HD), jnp.float32)
    (grad_keys, grad_values), grad_queries = lax.scan(
        one_block, (zero_heads, zero_heads), (query_blocks, grad_blocks, log_totals, starts)
    )
    return (
        grad_queries.reshape(extent, D),
        grad_keys.reshape(extent, D),
        grad_values.reshape(extent, D),
    )


def forward_micro(weights, inputs, segment):
    wide_qkv, wide_out, wide_fc, wide_proj, wide_vec = weights
    gain_one, bias_one, bias_query, bias_value, bias_out, gain_two, bias_two, bias_proj, bias_fc = (
        split_vectors(wide_vec.astype(jnp.float32))
    )
    extent = inputs.shape[0]
    normed_one = norm_rows(inputs, gain_one, bias_one).astype(jnp.bfloat16)
    bias_mixed = jnp.concatenate([bias_query, jnp.zeros_like(bias_query), bias_value])
    mixed_qkv = (
        jnp.dot(normed_one, wide_qkv, preferred_element_type=jnp.float32) + bias_mixed
    ).astype(jnp.bfloat16)
    queries = mixed_qkv[:, :D].reshape(extent, H, HD)
    keys_all = mixed_qkv[:, D : 2 * D].reshape(extent, H, HD)
    values_all = mixed_qkv[:, 2 * D :].reshape(extent, H, HD)
    attended, log_totals = attend_forward(queries, keys_all, values_all, segment)
    attended = attended.astype(jnp.bfloat16)
    middle = inputs + jnp.dot(attended, wide_out, preferred_element_type=jnp.float32) + bias_out
    normed_two = norm_rows(middle, gain_two, bias_two).astype(jnp.bfloat16)
    hidden_pre = jnp.dot(normed_two, wide_fc, preferred_element_type=jnp.float32) + bias_fc
    activated = gelu_tanh(hidden_pre).astype(jnp.bfloat16)
    result = middle + jnp.dot(activated, wide_proj, preferred_element_type=jnp.float32) + bias_proj
    kept_all = (
        normed_one,
        mixed_qkv,
        attended,
        log_totals,
        middle,
        normed_two,
        hidden_pre,
        activated,
    )
    return (result, kept_all)


def backward_micro(weights, inputs, kept_all, upstream, segment):
    wide_qkv, wide_out, wide_fc, wide_proj, wide_vec = weights
    gain_one, bias_one, bias_query, bias_value, bias_out, gain_two, bias_two, bias_proj, bias_fc = (
        split_vectors(wide_vec.astype(jnp.float32))
    )
    normed_one, mixed_qkv, attended, log_totals, middle, normed_two, hidden_pre, activated = (
        kept_all
    )
    extent = inputs.shape[0]
    grad_branch = upstream.astype(jnp.bfloat16)
    grad_proj = jnp.einsum("tf,td->fd", activated, grad_branch, preferred_element_type=jnp.float32)
    grad_bias_proj = jnp.sum(grad_branch.astype(jnp.float32), axis=0)
    grad_act = jnp.einsum("td,fd->tf", grad_branch, wide_proj, preferred_element_type=jnp.float32)
    _, gelu_back = jax.vjp(gelu_tanh, hidden_pre)
    grad_pre = gelu_back(grad_act)[0].astype(jnp.bfloat16)
    grad_fc = jnp.einsum("td,tf->df", normed_two, grad_pre, preferred_element_type=jnp.float32)
    grad_bias_fc = jnp.sum(grad_pre.astype(jnp.float32), axis=0)
    grad_normed_two = jnp.einsum("tf,df->td", grad_pre, wide_fc, preferred_element_type=jnp.float32)
    _, norm_back_two = jax.vjp(norm_rows, middle, gain_two, bias_two)
    grad_middle_part, grad_gain_two, grad_bias_two = norm_back_two(grad_normed_two)
    grad_middle = upstream + grad_middle_part
    grad_one = grad_middle.astype(jnp.bfloat16)
    grad_out = jnp.einsum("te,td->ed", attended, grad_one, preferred_element_type=jnp.float32)
    grad_bias_out = jnp.sum(grad_one.astype(jnp.float32), axis=0)
    grad_att = jnp.einsum(
        "td,ed->te", grad_one, wide_out, preferred_element_type=jnp.float32
    ).astype(jnp.bfloat16)
    queries = mixed_qkv[:, :D].reshape(extent, H, HD)
    keys_all = mixed_qkv[:, D : 2 * D].reshape(extent, H, HD)
    values_all = mixed_qkv[:, 2 * D :].reshape(extent, H, HD)
    grad_queries, grad_keys, grad_values = attend_backward(
        queries, keys_all, values_all, grad_att.reshape(extent, H, HD), log_totals, segment
    )
    grad_mixed = jnp.concatenate([grad_queries, grad_keys, grad_values], axis=1).astype(
        jnp.bfloat16
    )
    grad_qkv = jnp.einsum("td,te->de", normed_one, grad_mixed, preferred_element_type=jnp.float32)
    grad_bias_mixed = jnp.sum(grad_mixed.astype(jnp.float32), axis=0)
    grad_normed_one = jnp.einsum(
        "te,de->td", grad_mixed, wide_qkv, preferred_element_type=jnp.float32
    )
    _, norm_back_one = jax.vjp(norm_rows, inputs, gain_one, bias_one)
    grad_in_part, grad_gain_one, grad_bias_one = norm_back_one(grad_normed_one)
    grad_inputs = grad_middle + grad_in_part
    grad_vec = jnp.concatenate(
        [
            grad_gain_one,
            grad_bias_one,
            grad_bias_mixed[:D],
            grad_bias_mixed[2 * D :],
            grad_bias_out,
            grad_gain_two,
            grad_bias_two,
            grad_bias_proj,
            grad_bias_fc,
        ]
    )
    return ((grad_qkv, grad_out, grad_fc, grad_proj, grad_vec), grad_inputs)


def adamw_update(weight, moment_one, moment_two, gradient, step_rate, decay_rate):
    first_new = BETA_ONE * moment_one + (1.0 - BETA_ONE) * gradient
    second_new = BETA_TWO * moment_two + (1.0 - BETA_TWO) * gradient * gradient
    first_hat = first_new / (1.0 - BETA_ONE**STEP)
    second_hat = second_new / (1.0 - BETA_TWO**STEP)
    weight_new = weight - step_rate * (
        first_hat / (jnp.sqrt(second_hat) + EPS_ADAM) + decay_rate * weight
    )
    return (weight_new, first_new, second_new)


def per_device(
    tokens,
    cotangent,
    lengths,
    w_qkv,
    w_out,
    w_fc,
    w_proj,
    vectors,
    m_qkv,
    m_out,
    m_fc,
    m_proj,
    m_vectors,
    s_qkv,
    s_out,
    s_fc,
    s_proj,
    s_vectors,
):
    micro_count = lengths.shape[0]
    extent = tokens.shape[0] // micro_count
    low_qkv = w_qkv.astype(jnp.bfloat16)
    low_out = w_out.astype(jnp.bfloat16)
    low_fc = w_fc.astype(jnp.bfloat16)
    low_proj = w_proj.astype(jnp.bfloat16)
    low_vec = vectors.astype(jnp.bfloat16)
    inputs_all = tokens.astype(jnp.float32).reshape(micro_count, extent, D)
    upstream_all = cotangent.astype(jnp.float32).reshape(micro_count, extent, D)
    segments = [segment_ids(lengths[micro_index], extent) for micro_index in range(micro_count)]
    shared = (
        lax.all_gather(low_qkv, "fsdp", axis=0, tiled=True),
        lax.all_gather(low_out, "fsdp", axis=0, tiled=True),
        lax.all_gather(low_fc, "fsdp", axis=0, tiled=True),
        lax.all_gather(low_proj, "fsdp", axis=0, tiled=True),
        lax.all_gather(low_vec, "fsdp", axis=0, tiled=True),
    )
    results = []
    kept_list = []
    for micro_index in range(micro_count):
        weights_now = shared
        result, kept_all = forward_micro(
            weights_now, inputs_all[micro_index], segments[micro_index]
        )
        results.append(result)
        kept_list.append(kept_all)
    sums_all = None
    grad_rows = []
    for micro_index in range(micro_count):
        weights_now = shared
        grads_here, grad_inputs = backward_micro(
            weights_now,
            inputs_all[micro_index],
            kept_list[micro_index],
            upstream_all[micro_index],
            segments[micro_index],
        )
        if sums_all is None:
            sums_all = grads_here
        else:
            sums_all = tuple((total_g + new_g for total_g, new_g in zip(sums_all, grads_here)))
        grad_rows.append(grad_inputs)
    owned = (
        lax.psum_scatter(sums_all[0], "fsdp", scatter_dimension=0, tiled=True),
        lax.psum_scatter(sums_all[1], "fsdp", scatter_dimension=0, tiled=True),
        lax.psum_scatter(sums_all[2], "fsdp", scatter_dimension=0, tiled=True),
        lax.psum_scatter(sums_all[3], "fsdp", scatter_dimension=0, tiled=True),
        lax.psum_scatter(sums_all[4], "fsdp", scatter_dimension=0, tiled=True),
    )
    local_sum = jnp.zeros((), jnp.float32)
    for gradient in owned:
        local_sum = local_sum + jnp.sum(gradient * gradient)
    norm_total = jnp.sqrt(lax.psum(local_sum, "fsdp"))
    factor = THRESH / jnp.maximum(norm_total, THRESH)
    params = (w_qkv, w_out, w_fc, w_proj, vectors)
    firsts = (m_qkv, m_out, m_fc, m_proj, m_vectors)
    seconds = (s_qkv, s_out, s_fc, s_proj, s_vectors)
    new_weights = []
    new_firsts = []
    new_seconds = []
    for position in range(5):
        is_vector = position == 4
        step_rate = LR_VEC if is_vector else LR_MAT
        decay_rate = 0.0 if is_vector else WEIGHT_DECAY
        weight_new, first_new, second_new = adamw_update(
            params[position],
            firsts[position],
            seconds[position],
            owned[position] * factor,
            step_rate,
            decay_rate,
        )
        new_weights.append(weight_new)
        new_firsts.append(first_new)
        new_seconds.append(second_new)
    output = jnp.concatenate(results, axis=0).astype(jnp.bfloat16)
    input_grad = jnp.concatenate(grad_rows, axis=0)
    return (
        output,
        input_grad,
        norm_total,
        new_weights[0],
        new_weights[1],
        new_weights[2],
        new_weights[3],
        new_weights[4],
        new_firsts[0],
        new_firsts[1],
        new_firsts[2],
        new_firsts[3],
        new_firsts[4],
        new_seconds[0],
        new_seconds[1],
        new_seconds[2],
        new_seconds[3],
        new_seconds[4],
    )


def solution(mesh):
    in_specs = (
        P("fsdp", None),
        P("fsdp", None),
        P("fsdp", None),
        P("fsdp", None),
        P("fsdp", None),
        P("fsdp", None),
        P("fsdp", None),
        P("fsdp"),
        P("fsdp", None),
        P("fsdp", None),
        P("fsdp", None),
        P("fsdp", None),
        P("fsdp"),
        P("fsdp", None),
        P("fsdp", None),
        P("fsdp", None),
        P("fsdp", None),
        P("fsdp"),
    )
    out_specs = (
        P("fsdp", None),
        P("fsdp", None),
        P(),
        P("fsdp", None),
        P("fsdp", None),
        P("fsdp", None),
        P("fsdp", None),
        P("fsdp"),
        P("fsdp", None),
        P("fsdp", None),
        P("fsdp", None),
        P("fsdp", None),
        P("fsdp"),
        P("fsdp", None),
        P("fsdp", None),
        P("fsdp", None),
        P("fsdp", None),
        P("fsdp"),
    )
    return jax.shard_map(
        per_device, mesh=mesh, in_specs=in_specs, out_specs=out_specs, check_vma=False
    )
```

profile of v0, /device:TPU:0, one launch (start us, length us, event | category | flops | bytes accessed | tf_op | source)
XLA Modules:
  0.0 920.6 jit_solution(18173816546591408730)
XLA Ops:
  14.8 42.5 %all-reduce = bf16[9216]{0:T(1024)(128)(2,1)S(1)} all-reduce(bf16[9216]{0:T(1024)(128)(2,1)S(1)} %dynamic-update-slice), channel_id=1, replica_groups=mesh['fsdp'=32] {'fsdp'}, use_global_device_ids=true, to_apply=%add | all-reduce | flops 9216 | bytes 36864
  65.3 9.3 %all-gather.5.cloned.1.call-done = bf16[768,2304]{1,0:T(8,128)(2,1)} async-done(((bf16[24,2304]{1,0:T(8,128)(2,1)}), bf16[768,2304]{1,0:T(8,128)(2,1)}) %all-gather.5.cloned.1.call-update) | async-done | bytes 3538960 | tf_op jit(solution)/shard_map/all_gather | solution.py:272
  74.6 4.1 fusion.25
  87.1 4.1 fusion.24
  107.6 5.8 fusion.33
  113.4 17.5 %all-gather.7.cloned.1.call-done = bf16[768,768]{1,0:T(8,128)(2,1)} async-done(((bf16[24,768]{1,0:T(8,128)(2,1)}), bf16[768,768]{1,0:T(8,128)(2,1)}) %all-gather.7.cloned.1.call-update) | async-done | bytes 1179664 | tf_op jit(solution)/shard_map/all_gather | solution.py:273
  141.3 5.2 fusion.32
  149.0 48.0 %all-gather.9.cloned.1.call-done = bf16[768,3072]{1,0:T(8,128)(2,1)} async-done(((bf16[24,3072]{1,0:T(8,128)(2,1)}), bf16[768,3072]{1,0:T(8,128)(2,1)}) %all-gather.9.cloned.1.call-update) | async-done | bytes 4718608 | tf_op jit(solution)/shard_map/all_gather | solution.py:274
  197.0 8.1 fusion.64
  205.1 57.7 %all-gather.11.cloned.1.call-done = bf16[3072,768]{1,0:T(8,128)(2,1)} async-done(((bf16[96,768]{1,0:T(8,128)(2,1)}), bf16[3072,768]{1,0:T(8,128)(2,1)}) %all-gather.11.cloned.1.call-update) | async-done | bytes 4718608 | tf_op jit(solution)/shard_map/all_gather | solution.py:275
  262.8 10.1 %convert_reduce_fusion.1 = (f32[3072]{0:T(1024)}, bf16[512,3072]{1,0:T(8,128)(2,1)S(1)}) fusion(f32[512,3072]{1,0:T(8,128)} %fusion.64, f32[3072]{0:T(1024)S(1)} %slice.136, bf16[3072,768]{1,0:T(8,128)(2,1)} %all-gather.11.cloned.1.call-done, f32[1024,768]{1,0:T(8,128)} %convert_element_type.175), kind=kOutput, calls=%fused_computation.35 | convolution fusion | flops 2452091904 | bytes 14966784 | tf_op jit(solution)/shard_map/td,fd->tf/dot_general | solution.py:182
  278.9 7.1 convert_reduce_fusion
  286.1 3.8 multiply_reduce_fusion.2
  299.4 12.2 %multiply_reduce_fusion.1 = (f32[12,512]{1,0:T(8,128)S(1)}, f32[12,512,512]{1,2,0:T(8,128)}) fusion(f32[12,512]{1,0:T(8,128)S(1)} %log_add_fusion.1, f32[12,512,512]{1,2,0:T(8,128)} %copy-done, pred[512,512]{0,1:T(8,128)(4,1)} %fusion.35, bf16[512,12,64]{0,2,1:T(8,128)(2,1)} %bitcast.121, bf16[512,12,64]{0,2,1:T(8,128)(2,1)} %bitcast.120), kind=kOutput, calls=%fused_computation.4 | convolution fusion | flops 421521408 | bytes 27049984 | tf_op jit(solution)/shard_map/while/body/eval_jaxpr/qhd,khd->hqk/dot_general | solution.py:105
  311.6 7.1 multiply_convert_fusion.1
  327.8 11.7 %multiply_reduce_fusion = (f32[12,512]{1,0:T(8,128)S(1)}, f32[12,512,512]{1,2,0:T(8,128)}) fusion(f32[12,512]{1,0:T(8,128)S(1)} %log_add_fusion, f32[12,512,512]{1,2,0:T(8,128)} %copy-done.1, pred[512,512]{0,1:T(8,128)(4,1)S(1)} %fusion.34, bf16[512,12,64]{0,2,1:T(8,128)(2,1)} %bitcast.123, bf16[512,12,64]{0,2,1:T(8,128)(2,1)} %bitcast.118), kind=kOutput, calls=%fused_computation.1 | convolution fusion | flops 421521408 | bytes 27049984 | tf_op jit(solution)/shard_map/while/body/eval_jaxpr/qhd,khd->hqk/dot_general | solution.py:105
  340.8 7.1 multiply_convert_fusion
  355.3 8.3 fusion.26
  366.9 4.8 fusion.29
  372.6 5.2 convolution_add_fusion
  378.5 5.5 fusion.63
  384.0 5.8 convolution_add_fusion.2
  389.9 7.4 fusion.57
  397.3 10.3 %convolution_add_fusion.1 = f32[3072,768]{1,0:T(8,128)} fusion(f32[3072,768]{1,0:T(8,128)S(1)} %fusion.57, f32[1024,768]{1,0:T(8,128)S(1)} %copy-done.3, f32[512,3072]{1,0:T(8,128)} %copy-done.87, f32[3072]{0:T(1024)S(1)} %slice.136), kind=kOutput, calls=%fused_computation.45 | convolution fusion | flops 2434007040 | bytes 25964544 | tf_op jit(solution)/shard_map/tf,td->fd/dot_general | solution.py:180
  407.7 4.9 fusion.60
  421.0 40.1 %all-reduce.1 = f32[9216]{0:T(1024)S(1)} all-reduce(f32[9216]{0:T(1024)S(1)} %add.378), channel_id=6, replica_groups=mesh['fsdp'=32] {'fsdp'}, use_global_device_ids=true, to_apply=%region_50.51.clone | all-reduce | flops 9216 | bytes 73728
  463.9 9.3 %add_convert_fusion.3 = bf16[512,768]{1,0:T(8,128)(2,1)S(1)} fusion(f32[512,768]{1,0:T(8,128)S(1)} %copy-done.28, bf16[3072,768]{1,0:T(8,128)(2,1)} %all-gather.11.cloned.1.call-done, f32[768]{0:T(1024)S(1)} %copy-done.74, f32[512,3072]{1,0:T(8,128)} %fusion.64, f32[3072]{0:T(1024)S(1)} %slice.136), kind=kOutput, calls=%fused_computation.88 | convolution fusion | flops 2432827392 | bytes 13384704 | tf_op jit(solution)/shard_map/dot_general | solution.py:156
  473.3 4.0 add_convert_fusion
  479.0 98.8 %reduce-scatter.5.cloned.1.call-done = f32[24,2304]{1,0:T(8,128)} async-done(((f32[768,2304]{1,0:T(8,128)}), f32[24,2304]{1,0:T(8,128)}) %reduce-scatter.5.cloned.1.call-update) | async-done | bytes 221200 | tf_op jit(solution)/shard_map/reduce_scatter | solution.py:304
  580.7 137.8 %reduce-scatter.9.cloned.1.call-done = f32[24,3072]{1,0:T(8,128)} async-done(((f32[768,3072]{1,0:T(8,128)}), f32[24,3072]{1,0:T(8,128)}) %reduce-scatter.9.cloned.1.call-update) | async-done | bytes 294928 | tf_op jit(solution)/shard_map/reduce_scatter | solution.py:306
  720.8 139.3 %reduce-scatter.11.cloned.1.call-done = f32[96,768]{1,0:T(8,128)} async-done(((f32[3072,768]{1,0:T(8,128)}), f32[96,768]{1,0:T(8,128)}) %reduce-scatter.11.cloned.1.call-update) | async-done | bytes 294928 | tf_op jit(solution)/shard_map/reduce_scatter | solution.py:307
  864.4 39.6 %psum.7 = f32[]{:T(128)} all-reduce(f32[]{:T(128)S(6)} %add.379), channel_id=1, replica_groups=mesh['fsdp'=32] {'fsdp'}, use_global_device_ids=true, to_apply=%region_52.53 | all-reduce | flops 1 | bytes 8 | tf_op jit(solution)/shard_map/psum | solution.py:313
  (334 shorter events, 117.0 us)
Async XLA Ops:
  7.2 67.4 %all-gather.5.cloned.1.call-start = ((), (), s32[]{:S(2)}) async-start(), calls=%async_computation.4 | async-start | bytes 3649536 | tf_op jit(solution)/shard_map/all_gather | solution.py:272
  8.9 122.1 %all-gather.7.cloned.1.call-start = ((), (), s32[]{:S(2)}) async-start(), calls=%async_computation.5 | async-start | bytes 1216512 | tf_op jit(solution)/shard_map/all_gather | solution.py:273
  10.4 186.6 %all-gather.9.cloned.1.call-start = ((), (), s32[]{:S(2)}) async-start(), calls=%async_computation.6 | async-start | bytes 4866048 | tf_op jit(solution)/shard_map/all_gather | solution.py:274
  12.2 250.7 %all-gather.11.cloned.1.call-start = ((), (), s32[]{:S(2)}) async-start(), calls=%async_computation.7 | async-start | bytes 4866048 | tf_op jit(solution)/shard_map/all_gather | solution.py:275
  13.9 463.5 %reduce-scatter.7.cloned.1.call-start = ((), (), s32[]{:S(2)}) async-start(), calls=%async_computation.9 | async-start | bytes 2433024 | tf_op jit(solution)/shard_map/reduce_scatter | solution.py:305
  57.9 29.2 %copy-start.53 = (f32[768]{0:T(1024)}, f32[768]{0:T(1024)S(1)}, u32[]{:S(2)}) copy-start(f32[768]{0:T(1024)S(1)} %get-tuple-element.195) | copy-start | bytes 9220
  57.9 29.2 %copy-start.55 = (f32[768]{0:T(1024)}, f32[768]{0:T(1024)S(1)}, u32[]{:S(2)}) copy-start(f32[768]{0:T(1024)S(1)} %get-tuple-element.196) | copy-start | bytes 9220
  62.2 12.4 %copy-start.57 = (f32[512]{0:T(512)}, f32[512]{0:T(512)S(1)}, u32[]{:S(2)}) copy-start(f32[512]{0:T(512)S(1)} %get-tuple-element.224) | copy-start | bytes 6148
  62.2 24.9 %copy-start.61 = (f32[512]{0:T(512)}, f32[512]{0:T(512)S(1)}, u32[]{:S(2)}) copy-start(f32[512]{0:T(512)S(1)} %get-tuple-element.225) | copy-start | bytes 6148
  62.7 16.0 %copy-start.65 = (f32[512]{0:T(512)}, f32[512]{0:T(512)S(1)}, u32[]{:S(2)}) copy-start(f32[512]{0:T(512)S(1)} %get-tuple-element.134) | copy-start | bytes 6148
  63.2 23.9 %copy-start.69 = (f32[512]{0:T(512)}, f32[512]{0:T(512)S(1)}, u32[]{:S(2)}) copy-start(f32[512]{0:T(512)S(1)} %fusion.43) | copy-start | bytes 6148
  63.3 15.4 %copy-start.59 = (f32[512]{0:T(512)}, f32[512]{0:T(512)S(1)}, u32[]{:S(2)}) copy-start(f32[512]{0:T(512)S(1)} %fusion.45) | copy-start | bytes 6148
  148.9 141.0 %copy-start.71 = (f32[512]{0:T(512)}, f32[512]{0:T(512)S(1)}, u32[]{:S(2)}) copy-start(f32[512]{0:T(512)S(1)} %fusion.44) | copy-start | bytes 6148
  299.4 12.2 %slice-start.1 = ((s8[12582912]{0:T(1024)(128)(4,1)}), s8[4194304]{0:T(1024)(128)(4,1)S(1)}, s32[]{:S(2)}) async-start(s8[12582912]{0:T(1024)(128)(4,1)} %bitcast.86), calls=%async_computation.13 | async-start | bytes 8388608
  299.4 12.2 %slice-start.2 = ((s8[12582912]{0:T(1024)(128)(4,1)}), s8[4194304]{0:T(1024)(128)(4,1)S(1)}, s32[]{:S(2)}) async-start(s8[12582912]{0:T(1024)(128)(4,1)} %bitcast.86), calls=%async_computation.14 | async-start | bytes 8388608
  299.4 12.2 %copy-start.29 = (pred[512,512]{0,1:T(8,128)(4,1)S(1)}, pred[512,512]{0,1:T(8,128)(4,1)}, u32[]{:S(2)}) copy-start(pred[512,512]{0,1:T(8,128)(4,1)} %fusion.35) | copy-start | bytes 786436
  327.8 13.1 %slice-start.5 = ((s8[12582912]{0:T(1024)(128)(4,1)}), s8[4194304]{0:T(1024)(128)(4,1)S(1)}, s32[]{:S(2)}) async-start(s8[12582912]{0:T(1024)(128)(4,1)} %bitcast.88), calls=%async_computation.17 | async-start | bytes 8388608
  355.2 222.6 %reduce-scatter.5.cloned.1.call-start = ((), (), s32[]{:S(2)}) async-start(), calls=%async_computation.8 | async-start | bytes 7299072 | tf_op jit(solution)/shard_map/reduce_scatter | solution.py:304
  377.9 340.7 %reduce-scatter.9.cloned.1.call-start = ((), (), s32[]{:S(2)}) async-start(), calls=%async_computation.10 | async-start | bytes 9732096 | tf_op jit(solution)/shard_map/reduce_scatter | solution.py:306
  389.9 470.2 %reduce-scatter.11.cloned.1.call-start = ((), (), s32[]{:S(2)}) async-start(), calls=%async_computation.11 | async-start | bytes 9732096 | tf_op jit(solution)/shard_map/reduce_scatter | solution.py:307
  477.3 427.5 %copy-start.73 = (f32[288]{0:T(512)S(1)}, f32[288]{0:T(512)}, u32[]{:S(2)}) copy-start(f32[288]{0:T(512)} %param.25) | copy-start | bytes 3460
  477.3 427.5 %copy-start.79 = (f32[288]{0:T(512)S(1)}, f32[288]{0:T(512)}, u32[]{:S(2)}) copy-start(f32[288]{0:T(512)} %param.30) | copy-start | bytes 3460
  477.3 427.5 %copy-start.80 = (f32[288]{0:T(512)S(1)}, f32[288]{0:T(512)}, u32[]{:S(2)}) copy-start(f32[288]{0:T(512)} %param.35) | copy-start | bytes 3460
  477.3 429.9 %copy-start.44 = (f32[24,2304]{1,0:T(8,128)S(1)}, f32[24,2304]{1,0:T(8,128)}, u32[]{:S(2)}) copy-start(f32[24,2304]{1,0:T(8,128)} %param.21) | copy-start | bytes 663556
  477.3 431.8 %copy-start.39 = (f32[96,768]{1,0:T(8,128)S(1)}, f32[96,768]{1,0:T(8,128)}, u32[]{:S(2)}) copy-start(f32[96,768]{1,0:T(8,128)} %param.24) | copy-start | bytes 884740
  477.3 431.8 %copy-start.50 = (f32[96,768]{1,0:T(8,128)S(1)}, f32[96,768]{1,0:T(8,128)}, u32[]{:S(2)}) copy-start(f32[96,768]{1,0:T(8,128)} %param.29) | copy-start | bytes 884740
  577.8 329.4 %copy-start.43 = (f32[24,2304]{1,0:T(8,128)S(1)}, f32[24,2304]{1,0:T(8,128)}, u32[]{:S(2)}) copy-start(f32[24,2304]{1,0:T(8,128)} %reduce-scatter.5.cloned.1.call-done) | copy-start | bytes 663556
  860.1 49.1 %copy-start.42 = (f32[96,768]{1,0:T(8,128)S(1)}, f32[96,768]{1,0:T(8,128)}, u32[]{:S(2)}) copy-start(f32[96,768]{1,0:T(8,128)} %reduce-scatter.11.cloned.1.call-done) | copy-start | bytes 884740
  863.1 48.1 %copy-start.40 = (f32[24,3072]{1,0:T(8,128)S(1)}, f32[24,3072]{1,0:T(8,128)}, u32[]{:S(2)}) copy-start(f32[24,3072]{1,0:T(8,128)} %param.23) | copy-start | bytes 884740
  863.1 48.1 %copy-start.41 = (f32[24,3072]{1,0:T(8,128)S(1)}, f32[24,3072]{1,0:T(8,128)}, u32[]{:S(2)}) copy-start(f32[24,3072]{1,0:T(8,128)} %reduce-scatter.9.cloned.1.call-done) | copy-start | bytes 884740
  864.4 46.8 %copy-start.51 = (f32[24,3072]{1,0:T(8,128)S(1)}, f32[24,3072]{1,0:T(8,128)}, u32[]{:S(2)}) copy-start(f32[24,3072]{1,0:T(8,128)} %param.28) | copy-start | bytes 884740
  864.4 46.8 %copy-start.52 = (f32[24,3072]{1,0:T(8,128)S(1)}, f32[24,3072]{1,0:T(8,128)}, u32[]{:S(2)}) copy-start(f32[24,3072]{1,0:T(8,128)} %param.33) | copy-start | bytes 884740
  (78 other events, 371.5 us)
Sparse Core Ops, SparseCore 0:
  11.5 63.0 all-gather.4
  78.0 52.8 all-gather.6
  134.4 62.5 all-gather.8
  200.3 62.4 all-gather.10
  355.3 97.7 reduce-scatter.6
  459.6 118.1 reduce-scatter.4
  583.7 134.8 reduce-scatter.8
  725.4 134.6 reduce-scatter.10
where the time goes:
time: 931 us; the launch traced here: 921 us
  waiting for transfers between devices  509 us (55%)
  matrix products  175 us (19%)
  blocking collectives  122 us (13%)
  other arithmetic  57.9 us (6%)
  local copies, waits for them, and re-layouts  35.3 us (4%)
  between operations  21.1 us (2%)
    reduce_scatter x1, waiting for transfers between devices, per_device(): lax.psum_scatter(sums_all[3], 'fsdp', scatter_dimension=0, tiled=True)  139 us
    reduce_scatter x1, waiting for transfers between devices, per_device(): lax.psum_scatter(sums_all[2], 'fsdp', scatter_dimension=0, tiled=True)  138 us
    reduce_scatter x1, waiting for transfers between devices, per_device(): lax.psum_scatter(sums_all[0], 'fsdp', scatter_dimension=0, tiled=True)  98.8 us
    unnamed x2, blocking collectives  82.6 us
    all_gather x1, waiting for transfers between devices, per_device(): lax.all_gather(low_proj, 'fsdp', axis=0, tiled=True)  57.7 us
    all_gather x1, waiting for transfers between devices, per_device(): lax.all_gather(low_fc, 'fsdp', axis=0, tiled=True)  48 us
    psum x1, blocking collectives, per_device(): norm_total = jnp.sqrt(lax.psum(local_sum, 'fsdp'))  39.6 us
    dot_general x2, matrix products, one_block(): jnp.einsum('qhd,khd->hqk', grad_rows, values_all, preferred_element_type=...  23.9 us
  transfers between devices with their start and end apart: 8, of which 7 were waited for; matrix products, arithmetic and copies ran while one was open for 17% of the time, Pallas kernels for 0%

commit v1 on v0

v1 whole, which is shorter than its diff:
```python
import jax
import jax.numpy as jnp
from jax import lax
from jax.sharding import PartitionSpec as P

D = 768
H = 12
HD = 64
STEP = 10


EPS_NORM = 1e-05
THRESH = 1.0
BETA_ONE = 0.9
BETA_TWO = 0.999
LR_MAT = 0.03
LR_VEC = 0.5
WEIGHT_DECAY = 0.1
EPS_ADAM = 1e-08
BIG_NEG = -1e30


def segment_ids(lengths_row, extent):
    ends_all = jnp.cumsum(lengths_row)
    places = jnp.arange(extent, dtype=jnp.int32)
    return jnp.sum((places[:, None] >= ends_all[None, :]).astype(jnp.int32), axis=1)


def norm_rows(values_in, scaling, offset):
    center = values_in - jnp.mean(values_in, axis=-1, keepdims=True)
    variance = jnp.mean(center * center, axis=-1, keepdims=True)
    return center * lax.rsqrt(variance + EPS_NORM) * scaling + offset


def split_vectors(vec_all):
    pieces = [vec_all[position * D : (position + 1) * D] for position in range(8)]
    return pieces + [vec_all[8 * D :]]


def gelu_tanh(z):
    return jax.nn.gelu(z, approximate=True)


def block_mask(segment, start, block_rows, columns):
    rows_here = start + jnp.arange(block_rows, dtype=jnp.int32)
    return (segment[:, None] == segment[None, :]) & (rows_here[:, None] >= columns[None, :])


def attend_forward(queries, keys_all, values_all, segment):
    allowed = block_mask(segment, 0, segment.shape[0], jnp.arange(segment.shape[0]))
    scores = (
        jnp.einsum("qhd,khd->hqk", queries, keys_all, preferred_element_type=jnp.float32)
        * HD ** (-0.5)
    )
    scores = jnp.where(allowed[None], scores, BIG_NEG)
    highest = jnp.max(scores, axis=-1, keepdims=True)
    exponent = jnp.exp(scores - highest)
    totals = jnp.sum(exponent, axis=-1, keepdims=True)
    soft_probs = (exponent / totals).astype(jnp.bfloat16)
    attended = jnp.einsum(
        "hqk,khd->qhd", soft_probs, values_all, preferred_element_type=jnp.float32
    )
    return (attended.reshape(-1, D).astype(jnp.bfloat16), highest + jnp.log(totals))


def attend_backward(queries, keys_all, values_all, grad_rows, log_rows, segment):
    score_scale = HD ** (-0.5)
    allowed = block_mask(segment, 0, segment.shape[0], jnp.arange(segment.shape[0]))
    scores = (
        jnp.einsum("qhd,khd->hqk", queries, keys_all, preferred_element_type=jnp.float32)
        * score_scale
    )
    soft_probs = jnp.where(allowed[None], jnp.exp(scores - log_rows), 0.0)
    grad_values = jnp.einsum(
        "hqk,qhd->khd",
        soft_probs.astype(jnp.bfloat16),
        grad_rows,
        preferred_element_type=jnp.float32,
    )
    grad_probs = jnp.einsum(
        "qhd,khd->hqk", grad_rows, values_all, preferred_element_type=jnp.float32
    )
    grad_scores = soft_probs * (
        grad_probs - jnp.sum(soft_probs * grad_probs, axis=-1, keepdims=True)
    )
    grad_scores = grad_scores.astype(jnp.bfloat16)
    grad_query = (
        jnp.einsum("hqk,khd->qhd", grad_scores, keys_all, preferred_element_type=jnp.float32)
        * score_scale
    )
    grad_keys = (
        jnp.einsum("hqk,qhd->khd", grad_scores, queries, preferred_element_type=jnp.float32)
        * score_scale
    )
    return jnp.concatenate(
        [grad_query.reshape(-1, D), grad_keys.reshape(-1, D), grad_values.reshape(-1, D)], axis=1
    ).astype(jnp.bfloat16)


def all_attend_forward(mixed_qkv, lengths):
    micro_count = lengths.shape[0]
    extent = mixed_qkv.shape[0] // micro_count
    parts = []
    logs = []
    for index in range(micro_count):
        segment = segment_ids(lengths[index], extent)
        rows = mixed_qkv[index * extent : (index + 1) * extent]
        q, k, v = (rows[:, i * D : (i + 1) * D].reshape(extent, H, HD) for i in range(3))
        part, log_rows = attend_forward(q, k, v, segment)
        parts.append(part)
        logs.append(log_rows)
    return jnp.concatenate(parts, axis=0), logs


def all_attend_backward(mixed_qkv, grad_att, attended, logs, lengths):
    micro_count = lengths.shape[0]
    extent = mixed_qkv.shape[0] // micro_count
    parts = []
    for index in range(micro_count):
        segment = segment_ids(lengths[index], extent)
        rows = mixed_qkv[index * extent : (index + 1) * extent]
        q, k, v = (rows[:, i * D : (i + 1) * D].reshape(extent, H, HD) for i in range(3))
        grads = grad_att[index * extent : (index + 1) * extent].reshape(extent, H, HD)
        parts.append(attend_backward(q, k, v, grads, logs[index], segment))
    return jnp.concatenate(parts, axis=0)


def flip_pairs(count, bit):
    return [(place, place ^ (1 << bit)) for place in range(count)]


def spread_orders(count):
    far = list(range(count.bit_length() - 2, 0, -1))
    swapped = far[:-2] + far[-2:][::-1]
    moved = far[:1] + far[2:] + far[1:2]
    return far + [0], swapped + [0], moved + [0]


def gather_rows(piece, order, count):
    me = lax.axis_index("fsdp")
    held = []
    current = piece
    for bit in order:
        other = lax.ppermute(current, "fsdp", flip_pairs(count, bit))
        axis = sum(1 for known in held if known > bit)
        mine_high = ((me >> bit) & 1) == 1
        low = jnp.where(mine_high, other, current)
        high = jnp.where(mine_high, current, other)
        current = jnp.stack([low, high], axis=axis)
        held.append(bit)
    return current.reshape((count * piece.shape[0],) + piece.shape[1:])


class RowSum:
    def __init__(self, total, order, count, kind):
        rows = total.shape[0] // count
        self.bits = list(range(count.bit_length() - 2, -1, -1))
        self.current = total.reshape((2,) * len(self.bits) + (rows,) + total.shape[1:])
        self.order = list(order)
        self.count = count
        self.kind = kind

    def first_send(self):
        return self.half(self.order[0], 1).astype(self.kind)

    def half(self, bit, flipped):
        mine = ((lax.axis_index("fsdp") >> bit) & 1) ^ flipped
        return lax.dynamic_index_in_dim(
            self.current, mine, axis=self.bits.index(bit), keepdims=False
        )

    def finish(self, sent):
        for position, bit in enumerate(self.order):
            if position > 0:
                sent = self.half(bit, 1).astype(self.kind)
            arrived = lax.ppermute(sent, "fsdp", flip_pairs(self.count, bit))
            self.current = self.half(bit, 0) + arrived.astype(jnp.float32)
            self.bits.remove(bit)
        return self.current


def sum_all(value, count):
    total = jnp.full((8, 128), value, jnp.float32)
    for bit in range(count.bit_length() - 1):
        total = total + lax.ppermute(total, "fsdp", flip_pairs(count, bit))
    return total[0, 0]


def adamw_update(weight, moment_one, moment_two, gradient, step_rate, decay_rate):
    first_new = BETA_ONE * moment_one + (1.0 - BETA_ONE) * gradient
    second_new = BETA_TWO * moment_two + (1.0 - BETA_TWO) * gradient * gradient
    first_hat = first_new / (1.0 - BETA_ONE**STEP)
    second_hat = second_new / (1.0 - BETA_TWO**STEP)
    weight_new = weight - step_rate * (
        first_hat / (jnp.sqrt(second_hat) + EPS_ADAM) + decay_rate * weight
    )
    return (weight_new, first_new, second_new)


def per_device(
    tokens,
    cotangent,
    lengths,
    w_qkv,
    w_out,
    w_fc,
    w_proj,
    vectors,
    m_qkv,
    m_out,
    m_fc,
    m_proj,
    m_vectors,
    s_qkv,
    s_out,
    s_fc,
    s_proj,
    s_vectors,
):
    count = lax.axis_size("fsdp")
    order_one, order_two, order_three = spread_orders(count)
    low_vec = gather_rows(vectors.astype(jnp.bfloat16).reshape(1, -1), order_one, count)
    wide_qkv = gather_rows(w_qkv.astype(jnp.bfloat16), order_one, count)
    wide_out = gather_rows(w_out.astype(jnp.bfloat16), order_two, count)
    wide_fc = gather_rows(w_fc.astype(jnp.bfloat16), order_two, count)
    wide_proj = gather_rows(w_proj.astype(jnp.bfloat16), order_three, count)
    gain_one, bias_one, bias_query, bias_value, bias_out, gain_two, bias_two, bias_proj, bias_fc = (
        split_vectors(low_vec.reshape(-1).astype(jnp.float32))
    )
    inputs = tokens.astype(jnp.float32)
    normed_one = norm_rows(inputs, gain_one, bias_one).astype(jnp.bfloat16)
    bias_mixed = jnp.concatenate([bias_query, jnp.zeros_like(bias_query), bias_value])
    mixed_qkv = (
        jnp.dot(normed_one, wide_qkv, preferred_element_type=jnp.float32) + bias_mixed
    ).astype(jnp.bfloat16)
    attended, logs = all_attend_forward(mixed_qkv, lengths)
    middle = inputs + jnp.dot(attended, wide_out, preferred_element_type=jnp.float32) + bias_out
    normed_two = norm_rows(middle, gain_two, bias_two).astype(jnp.bfloat16)
    hidden_pre = jnp.dot(normed_two, wide_fc, preferred_element_type=jnp.float32) + bias_fc
    activated = gelu_tanh(hidden_pre).astype(jnp.bfloat16)

    upstream = cotangent.astype(jnp.float32)
    grad_proj = jnp.einsum("tf,td->fd", activated, cotangent, preferred_element_type=jnp.float32)
    sum_proj = RowSum(grad_proj, order_three[::-1], count, jnp.bfloat16)
    send_proj = sum_proj.first_send()
    grad_act = jnp.einsum("td,fd->tf", cotangent, wide_proj, preferred_element_type=jnp.float32)
    _, gelu_back = jax.vjp(gelu_tanh, hidden_pre)
    grad_pre = gelu_back(grad_act)[0].astype(jnp.bfloat16)
    grad_pre, send_proj = lax.optimization_barrier((grad_pre, send_proj))
    result = middle + jnp.dot(activated, wide_proj, preferred_element_type=jnp.float32) + bias_proj
    output = result.astype(jnp.bfloat16)
    grad_fc = jnp.einsum("td,tf->df", normed_two, grad_pre, preferred_element_type=jnp.float32)
    sum_fc = RowSum(grad_fc, order_two[::-1], count, jnp.bfloat16)
    send_fc = sum_fc.first_send()
    grad_normed_two = jnp.einsum("tf,df->td", grad_pre, wide_fc, preferred_element_type=jnp.float32)
    _, norm_back_two = jax.vjp(norm_rows, middle, gain_two, bias_two)
    grad_middle_part, grad_gain_two, grad_bias_two = norm_back_two(grad_normed_two)
    grad_middle = upstream + grad_middle_part
    grad_one = grad_middle.astype(jnp.bfloat16)
    grad_out = jnp.einsum("te,td->ed", attended, grad_one, preferred_element_type=jnp.float32)
    sum_out = RowSum(grad_out, order_one[::-1], count, jnp.bfloat16)
    send_out = sum_out.first_send()
    grad_att = jnp.einsum(
        "td,ed->te", grad_one, wide_out, preferred_element_type=jnp.float32
    ).astype(jnp.bfloat16)
    grad_att, send_fc, send_out = lax.optimization_barrier((grad_att, send_fc, send_out))
    grad_mixed = all_attend_backward(mixed_qkv, grad_att, attended, logs, lengths)
    grad_qkv = jnp.einsum("td,te->de", normed_one, grad_mixed, preferred_element_type=jnp.float32)
    width = grad_qkv.shape[1] // 2
    sum_left = RowSum(grad_qkv[:, :width], order_one[::-1], count, jnp.bfloat16)
    sum_right = RowSum(grad_qkv[:, width:], order_two[::-1], count, jnp.bfloat16)
    send_left = sum_left.first_send()
    send_right = sum_right.first_send()
    grad_mixed, send_left, send_right = lax.optimization_barrier(
        (grad_mixed, send_left, send_right)
    )
    grad_normed_one = jnp.einsum(
        "te,de->td", grad_mixed, wide_qkv, preferred_element_type=jnp.float32
    )
    _, norm_back_one = jax.vjp(norm_rows, inputs, gain_one, bias_one)
    grad_in_part, grad_gain_one, grad_bias_one = norm_back_one(grad_normed_one)
    input_grad = grad_middle + grad_in_part
    grad_bias_mixed = jnp.sum(grad_mixed.astype(jnp.float32), axis=0)
    grad_vec = jnp.concatenate(
        [
            grad_gain_one,
            grad_bias_one,
            grad_bias_mixed[:D],
            grad_bias_mixed[2 * D :],
            jnp.sum(grad_one.astype(jnp.float32), axis=0),
            grad_gain_two,
            grad_bias_two,
            jnp.sum(upstream, axis=0),
            jnp.sum(grad_pre.astype(jnp.float32), axis=0),
        ]
    )
    sum_vec = RowSum(grad_vec.reshape(count, -1), order_one[::-1], count, jnp.float32)
    owned_proj = sum_proj.finish(send_proj)
    owned_fc = sum_fc.finish(send_fc)
    owned_out = sum_out.finish(send_out)
    owned_qkv = jnp.concatenate(
        [sum_left.finish(send_left), sum_right.finish(send_right)], axis=1
    )
    owned_vec = sum_vec.finish(sum_vec.first_send()).reshape(-1)
    owned = (owned_qkv, owned_out, owned_fc, owned_proj, owned_vec)
    local_sum = jnp.zeros((), jnp.float32)
    for gradient in owned:
        local_sum = local_sum + jnp.sum(gradient * gradient)
    norm_total = jnp.sqrt(sum_all(local_sum, count))
    factor = THRESH / jnp.maximum(norm_total, THRESH)
    params = (w_qkv, w_out, w_fc, w_proj, vectors)
    firsts = (m_qkv, m_out, m_fc, m_proj, m_vectors)
    seconds = (s_qkv, s_out, s_fc, s_proj, s_vectors)
    new_weights = []
    new_firsts = []
    new_seconds = []
    for position in range(5):
        is_vector = position == 4
        step_rate = LR_VEC if is_vector else LR_MAT
        decay_rate = 0.0 if is_vector else WEIGHT_DECAY
        weight_new, first_new, second_new = adamw_update(
            params[position],
            firsts[position],
            seconds[position],
            owned[position] * factor,
            step_rate,
            decay_rate,
        )
        new_weights.append(weight_new)
        new_firsts.append(first_new)
        new_seconds.append(second_new)
    return (
        output,
        input_grad,
        norm_total,
        new_weights[0],
        new_weights[1],
        new_weights[2],
        new_weights[3],
        new_weights[4],
        new_firsts[0],
        new_firsts[1],
        new_firsts[2],
        new_firsts[3],
        new_firsts[4],
        new_seconds[0],
        new_seconds[1],
        new_seconds[2],
        new_seconds[3],
        new_seconds[4],
    )


def solution(mesh):
    in_specs = (
        P("fsdp", None),
        P("fsdp", None),
        P("fsdp", None),
        P("fsdp", None),
        P("fsdp", None),
        P("fsdp", None),
        P("fsdp", None),
        P("fsdp"),
        P("fsdp", None),
        P("fsdp", None),
        P("fsdp", None),
        P("fsdp", None),
        P("fsdp"),
        P("fsdp", None),
        P("fsdp", None),
        P("fsdp", None),
        P("fsdp", None),
        P("fsdp"),
    )
    out_specs = (
        P("fsdp", None),
        P("fsdp", None),
        P(),
        P("fsdp", None),
        P("fsdp", None),
        P("fsdp", None),
        P("fsdp", None),
        P("fsdp"),
        P("fsdp", None),
        P("fsdp", None),
        P("fsdp", None),
        P("fsdp", None),
        P("fsdp"),
        P("fsdp", None),
        P("fsdp", None),
        P("fsdp", None),
        P("fsdp", None),
        P("fsdp"),
    )
    return jax.shard_map(
        per_device, mesh=mesh, in_specs=in_specs, out_specs=out_specs, check_vma=False
    )
```

time: 931 us -> 545 us (0.59)
  waiting for transfers between devices: 509 us -> 140 us
  blocking collectives: 122 us -> 0 us
  starting transfers between devices: 0.33 us -> 62.2 us
  other arithmetic: 57.9 us -> 115 us
  local copies, waits for them, and re-layouts: 35.3 us -> 76.5 us
  matrix products: 175 us -> 135 us
  between operations: 21.1 us -> 8.14 us
    reduce_scatter x4 -> x0, waiting for transfers between devices: 376 us -> none  [the longest x1 139 us: per_device(): lax.psum_scatter(sums_all[3], 'fsdp', scatter_dimension=0, tiled=True)]
    ppermute x0 -> x60, waiting for transfers between devices: none -> 140 us  [the longest x30 81 us: finish(): arrived = lax.ppermute(sent, 'fsdp', flip_pairs(self.count, bit))]
    all_gather x4 -> x0, waiting for transfers between devices: 133 us -> none  [the longest x1 57.7 us: per_device(): lax.all_gather(low_proj, 'fsdp', axis=0, tiled=True)]
    unnamed x2 -> x0, blocking collectives: 82.6 us -> none
    ppermute x0 -> x60, starting transfers between devices: none -> 62.2 us  [the longest x25 30.6 us: gather_rows(): other = lax.ppermute(current, 'fsdp', flip_pairs(count, bit))]
    dot_general x36 -> x24, matrix products: 175 us -> 135 us  [the longest x2 18.9 us: attend_backward(): jnp.einsum('qhd,khd->hqk', grad_rows, values_all, preferred_element_type=...]
    psum x1 -> x0, blocking collectives: 39.6 us -> none  [per_device(): norm_total = jnp.sqrt(lax.psum(local_sum, 'fsdp'))]
    concatenate x3 -> x2, other arithmetic: 3.12 us -> 28.3 us  [the longest x1 28.3 us: all_attend_backward(): return jnp.concatenate(parts, axis=0)]
  transfers between devices with their start and end apart: 8 -> 60, of which waited for: 7 -> 33; matrix products, arithmetic and copies ran while one was open for 17% -> 19% of each run, Pallas kernels for 0% -> 0%
where the time goes in v1:
time: 545 us; the launch traced here: 536 us
  waiting for transfers between devices  140 us (26%)
  matrix products  135 us (25%)
  other arithmetic  115 us (21%)
  local copies, waits for them, and re-layouts  76.5 us (14%)
  starting transfers between devices  62.2 us (11%)
  between operations  8.14 us (1%)
    ppermute x30, waiting for transfers between devices, finish(): arrived = lax.ppermute(sent, 'fsdp', flip_pairs(self.count, bit))  81 us
    ppermute x25, waiting for transfers between devices, gather_rows(): other = lax.ppermute(current, 'fsdp', flip_pairs(count, bit))  49.8 us
    unnamed x202, local copies, waits for them, and re-layouts  33.1 us
    ppermute x25, starting transfers between devices, gather_rows(): other = lax.ppermute(current, 'fsdp', flip_pairs(count, bit))  30.6 us
    concatenate x1, other arithmetic, all_attend_backward(): return jnp.concatenate(parts, axis=0)  28.3 us
    ppermute x30, starting transfers between devices, finish(): arrived = lax.ppermute(sent, 'fsdp', flip_pairs(self.count, bit))  27.9 us
    dot_general x2, matrix products, attend_backward(): jnp.einsum('qhd,khd->hqk', grad_rows, values_all, preferred_element_type=...  18.9 us
    another operation x49, other arithmetic, gather_rows(): current = jnp.stack([low, high], axis=axis)  16.1 us
  transfers between devices with their start and end apart: 60, of which 33 were waited for; matrix products, arithmetic and copies ran while one was open for 19% of the time, Pallas kernels for 0%

profile of v1, /device:TPU:0, one launch (start us, length us, event | category | flops | bytes accessed | tf_op | source)
XLA Modules:
  0.0 536.4 jit_solution(9370829208267068595)
XLA Ops:
  1.3 4.0 collective-permute-start
  55.6 3.9 collective-permute-done.13
  59.7 7.4 %collective-permute-done.7 = bf16[2,2,24,2304]{3,2,1,0:T(8,128)(2,1)S(1)} collective-permute-done((bf16[2,2,24,2304]{3,2,1,0:T(8,128)(2,1)S(1)}, bf16[2,2,24,2304]{3,2,1,0:T(8,128)(2,1)S(1)}, u32[]{:S(2)}, u32[]{:S(2)}) %collective-permute-start.7) | collective-permute-done | bytes 442400 | tf_op jit(solution)/shard_map/ppermute | solution.py:144
  70.5 11.8 %collective-permute-done.17 = bf16[2,2,24,3072]{3,2,1,0:T(8,128)(2,1)S(1)} collective-permute-done((bf16[2,2,24,3072]{3,2,1,0:T(8,128)(2,1)S(1)}, bf16[2,2,24,3072]{3,2,1,0:T(8,128)(2,1)S(1)}, u32[]{:S(2)}, u32[]{:S(2)}) %collective-permute-start.17) | collective-permute-done | bytes 589856 | tf_op jit(solution)/shard_map/ppermute | solution.py:144
  84.1 12.3 %collective-permute-done.8 = bf16[2,2,2,24,2304]{4,3,2,1,0:T(8,128)(2,1)S(1)} collective-permute-done((bf16[2,2,2,24,2304]{4,3,2,1,0:T(8,128)(2,1)S(1)}, bf16[2,2,2,24,2304]{4,3,2,1,0:T(8,128)(2,1)S(1)}, u32[]{:S(2)}, u32[]{:S(2)}) %collective-permute-start.8) | collective-permute-done | bytes 884768 | tf_op jit(solution)/shard_map/ppermute | solution.py:144
  104.6 4.8 add_convert_fusion
  130.8 5.8 %fusion.44 = bf16[12,64,512]{2,1,0:T(8,128)(2,1)} fusion(bf16[512,12,64]{0,2,1:T(8,128)(2,1)} %bitcast.419, f32[12,512,512]{1,2,0:T(8,128)S(1)} %get-tuple-element.186, f32[12,512]{1,0:T(8,128)S(1)} %fusion.10, f32[12,512]{1,0:T(8,128)S(1)} %get-tuple-element.185, pred[512,512]{0,1:T(8,128)(4,1)S(1)} %fusion.48), kind=kOutput, calls=%fused_computation.103 | convolution fusion | flops 418775040 | bytes 14467072 | tf_op jit(solution)/shard_map/hqk,khd->qhd/dot_general | solution.py:60
  143.3 4.1 fusion.43
  158.9 5.5 %fusion.115 = f32[1024,3072]{1,0:T(8,128)S(1)} fusion(bf16[768,3072]{1,0:T(8,128)(2,1)S(1)} %bitcast.391, f32[1024,768]{0,1:T(8,128)S(1)} %get-tuple-element.188, f32[768]{0:T(1024)S(1)} %get-tuple-element.165, f32[768]{0:T(1024)S(1)} %get-tuple-element.163, f32[1024]{0:T(1024)S(1)} %fusion.87, f32[1024]{0:T(1024)S(1)} %broadcast_multiply_fusion), kind=kOutput, calls=%fused_computation.343 | convolution fusion | flops 4835770368 | bytes 20461568 | tf_op jit(solution)/shard_map/dot_general | solution.py:239
  164.5 10.4 %fusion.116 = f32[3072,768]{1,0:T(8,128)} fusion(bf16[1024,768]{1,0:T(8,128)(2,1)S(1)} %copy-done.52, f32[1024,3072]{1,0:T(8,128)S(1)} %fusion.115, f32[3072]{0:T(1024)S(1)} %slice.127), kind=kOutput, calls=%fused_computation.344 | convolution fusion | flops 4863295488 | bytes 23605248 | tf_op jit(solution)/shard_map/tf,td->fd/dot_general | solution.py:243
  174.9 15.2 %fusion.6 = bf16[1024,3072]{1,0:T(8,128)(2,1)} fusion(f32[1024,3072]{1,0:T(8,128)S(1)} %fusion.115, f32[3072]{0:T(1024)S(1)} %slice.127, bf16[3072,768]{1,0:T(8,128)(2,1)} %bitcast.415, bf16[1024,768]{1,0:T(8,128)(2,1)S(1)} %copy-done.52), kind=kOutput, calls=%fused_computation.8 | convolution fusion | flops 4897898496 | bytes 25178112 | tf_op jit(solution)/shard_map/td,fd->tf/dot_general | solution.py:246
  190.1 4.2 fusion.34
  194.3 9.3 %fusion.130 = (f32[768]{0:T(1024)}, f32[1024,768]{1,0:T(8,128)}) fusion(bf16[1024,3072]{1,0:T(8,128)(2,1)} %fusion.6, bf16[768,3072]{1,0:T(8,128)(2,1)S(1)} %bitcast.392), kind=kOutput, calls=%fused_computation.352 | convolution fusion | flops 4832623616 | bytes 14158848 | tf_op jit(solution)/shard_map/tf,df->td/dot_general | solution.py:255
  204.5 7.9 %fusion.114 = f32[768,3072]{1,0:T(8,128)} fusion(bf16[1024,3072]{1,0:T(8,128)(2,1)S(1)} %bitcast.408, f32[1024,768]{0,1:T(8,128)S(1)} %get-tuple-element.188, f32[768]{0:T(1024)S(1)} %get-tuple-element.165, f32[768]{0:T(1024)S(1)} %get-tuple-element.163, f32[1024]{0:T(1024)S(1)} %fusion.87, f32[1024]{0:T(1024)S(1)} %broadcast_multiply_fusion), kind=kOutput, calls=%fused_computation.342 | convolution fusion | flops 4835770368 | bytes 18888704 | tf_op jit(solution)/shard_map/td,tf->df/dot_general | solution.py:252
  225.8 5.0 fusion.35
  232.2 7.1 %fusion.40 = bf16[12,64,512]{2,1,0:T(8,128)(2,1)} fusion(bf16[512,12,64]{0,2,1:T(8,128)(2,1)S(1)} %bitcast.423, f32[12,512,512]{1,2,0:T(8,128)} %copy-done.1, f32[12,512]{1,0:T(8,128)S(1)} %log_add_fusion, pred[512,512]{0,1:T(8,128)(4,1)S(1)} %copy-done.36), kind=kOutput, calls=%fused_computation.101 | convolution fusion | flops 415629312 | bytes 14442496 | tf_op jit(solution)/shard_map/hqk,qhd->khd/dot_general | solution.py:74
  239.3 9.4 %multiply_reduce_fusion = (f32[12,512]{1,0:T(8,128)S(1)}, f32[12,512,512]{1,2,0:T(8,128)}) fusion(f32[12,512,512]{1,2,0:T(8,128)} %copy-done.1, f32[12,512]{1,0:T(8,128)S(1)} %log_add_fusion, pred[512,512]{0,1:T(8,128)(4,1)S(1)} %copy-done.36, bf16[512,12,64]{0,2,1:T(8,128)(2,1)S(1)} %bitcast.424, bf16[512,12,64]{0,2,1:T(8,128)(2,1)S(1)} %bitcast.422), kind=kOutput, calls=%fused_computation.16 | convolution fusion | flops 418375680 | bytes 27049984 | tf_op jit(solution)/shard_map/qhd,khd->hqk/dot_general | solution.py:80
  248.7 7.4 %multiply_convert_fusion = bf16[12,512,512]{1,2,0:T(8,128)(2,1)S(1)} fusion(f32[12,512,512]{1,2,0:T(8,128)} %get-tuple-element.190, f32[12,512,512]{1,2,0:T(8,128)S(1)} %bitcast.390, f32[12,512]{1,0:T(8,128)S(1)} %get-tuple-element.189, f32[12,512]{1,0:T(8,128)S(1)} %log_add_fusion, pred[512,512]{0,1:T(8,128)(4,1)S(1)} %copy-done.36), kind=kLoop, calls=%fused_computation.15 | loop fusion | flops 18874368 | bytes 31768576 | tf_op jit(solution)/shard_map/convert_element_type | solution.py:86
  260.4 7.2 %fusion.37 = bf16[12,64,512]{2,1,0:T(8,128)(2,1)} fusion(bf16[512,12,64]{0,2,1:T(8,128)(2,1)S(1)} %bitcast.425, f32[12,512,512]{1,2,0:T(8,128)} %copy-done, f32[12,512]{1,0:T(8,128)S(1)} %log_add_fusion.1, pred[512,512]{0,1:T(8,128)(4,1)S(1)} %fusion.48), kind=kOutput, calls=%fused_computation.100 | convolution fusion | flops 415629312 | bytes 14442496 | tf_op jit(solution)/shard_map/hqk,qhd->khd/dot_general | solution.py:74
  267.6 9.5 %multiply_reduce_fusion.1 = (f32[12,512]{1,0:T(8,128)S(1)}, f32[12,512,512]{1,2,0:T(8,128)}) fusion(f32[12,512,512]{1,2,0:T(8,128)} %copy-done, f32[12,512]{1,0:T(8,128)S(1)} %log_add_fusion.1, pred[512,512]{0,1:T(8,128)(4,1)S(1)} %fusion.48, bf16[512,12,64]{0,2,1:T(8,128)(2,1)S(1)} %bitcast.426, bf16[512,12,64]{0,2,1:T(8,128)(2,1)S(1)} %bitcast.420), kind=kOutput, calls=%fused_computation.19 | convolution fusion | flops 418375680 | bytes 27049984 | tf_op jit(solution)/shard_map/qhd,khd->hqk/dot_general | solution.py:80
  277.2 7.1 %multiply_convert_fusion.1 = bf16[12,512,512]{1,2,0:T(8,128)(2,1)S(1)} fusion(f32[12,512,512]{1,2,0:T(8,128)} %get-tuple-element.192, f32[12,512,512]{1,2,0:T(8,128)S(1)} %bitcast.388, f32[12,512]{1,0:T(8,128)S(1)} %get-tuple-element.191, f32[12,512]{1,0:T(8,128)S(1)} %log_add_fusion.1, pred[512,512]{0,1:T(8,128)(4,1)S(1)} %fusion.48), kind=kLoop, calls=%fused_computation.18 | loop fusion | flops 18874368 | bytes 31768576 | tf_op jit(solution)/shard_map/convert_element_type | solution.py:86
  287.9 28.3 %maximum_maximum_fusion = bf16[1024,2304]{0,1:T(8,128)(2,1)S(1)} fusion(bf16[512,768]{0,1:T(8,128)(2,1)S(1)} %bitcast.433, bf16[512,768]{0,1:T(8,128)(2,1)S(1)} %bitcast.427, bf16[512,768]{0,1:T(8,128)(2,1)S(1)} %bitcast.405, bf16[512,768]{0,1:T(8,128)(2,1)S(1)} %bitcast.434, bf16[512,768]{0,1:T(8,128)(2,1)S(1)} %bitcast.428, bf16[512,768]{0,1:T(8,128)(2,1)S(1)} %bitcast.406), kind=kLoop, calls=%fused_computation.51 | loop fusion | flops 28311552 | bytes 9437184 | tf_op jit(solution)/shard_map/concatenate | solution.py:125
  316.2 4.1 fusion.111
  325.5 5.6 %fusion.129 = (f32[768]{0:T(1024)S(1)}, f32[1024,768]{1,0:T(8,128)}) fusion(bf16[1024,2304]{0,1:T(8,128)(2,1)S(1)} %maximum_maximum_fusion, bf16[768,2304]{1,0:T(8,128)(2,1)S(1)} %bitcast.418), kind=kOutput, calls=%fused_computation.351 | convolution fusion | flops 3624664320 | bytes 11406336 | tf_op jit(solution)/shard_map/te,de->td/dot_general | solution.py:277
  399.2 6.1 %collective-permute-done.31 = bf16[2,2,2,24,1152]{4,3,0,1,2:T(8,128)(2,1)S(1)} collective-permute-done((bf16[2,2,2,24,1152]{4,3,0,1,2:T(8,128)(2,1)S(1)}, bf16[2,2,2,24,1152]{4,3,0,1,2:T(8,128)(2,1)S(1)}, u32[]{:S(2)}, u32[]{:S(2)}) %collective-permute-start.31) | collective-permute-done | bytes 442400 | tf_op jit(solution)/shard_map/ppermute | solution.py:176
  422.3 21.0 %collective-permute-done.46 = bf16[2,2,2,96,768]{4,3,0,1,2:T(8,128)(2,1)S(1)} collective-permute-done((bf16[2,2,2,96,768]{4,3,0,1,2:T(8,128)(2,1)S(1)}, bf16[2,2,2,96,768]{4,3,0,1,2:T(8,128)(2,1)S(1)}, u32[]{:S(2)}, u32[]{:S(2)}) %collective-permute-start.46) | collective-permute-done | bytes 1179680 | tf_op jit(solution)/shard_map/ppermute | solution.py:176
  446.2 13.7 %collective-permute-done.47 = bf16[2,2,96,768]{3,2,0,1:T(8,128)(2,1)S(1)} collective-permute-done((bf16[2,2,96,768]{3,2,0,1:T(8,128)(2,1)S(1)}, bf16[2,2,96,768]{3,2,0,1:T(8,128)(2,1)S(1)}, u32[]{:S(2)}, u32[]{:S(2)}) %collective-permute-start.47) | collective-permute-done | bytes 589856 | tf_op jit(solution)/shard_map/ppermute | solution.py:176
  461.0 7.5 %collective-permute-done.42 = bf16[2,2,24,3072]{3,2,0,1:T(8,128)(2,1)S(1)} collective-permute-done((bf16[2,2,24,3072]{3,2,0,1:T(8,128)(2,1)S(1)}, bf16[2,2,24,3072]{3,2,0,1:T(8,128)(2,1)S(1)}, u32[]{:S(2)}, u32[]{:S(2)}) %collective-permute-start.42) | collective-permute-done | bytes 589856 | tf_op jit(solution)/shard_map/ppermute | solution.py:176
  469.6 4.0 collective-permute-start.49
  473.6 4.7 collective-permute-done.43
  482.0 4.9 collective-permute-done.44
  505.4 12.0 %add_convert_fusion.1 = bf16[1024,768]{0,1:T(8,128)(2,1)} fusion(f32[1024,768]{0,1:T(8,128)S(1)} %copy-done.6, bf16[3072,768]{1,0:T(8,128)(2,1)} %bitcast.416, f32[768]{0:T(1024)} %get-tuple-element.164, f32[1024,3072]{1,0:T(8,128)} %copy-done.13, f32[3072]{0:T(1024)} %copy-done.75), kind=kOutput, calls=%fused_computation.71 | convolution fusion | flops 4865654784 | bytes 22035456 | tf_op jit(solution)/shard_map/dot_general | solution.py:250
  (502 shorter events, 257.2 us)
Async XLA Ops:
  1.3 17.9 %collective-permute-start = (bf16[1,288]{1,0:T(2,128)(2,1)S(1)}, bf16[1,288]{1,0:T(2,128)(2,1)S(1)}, u32[]{:S(2)}, u32[]{:S(2)}) collective-permute-start(bf16[1,288]{1,0:T(2,128)(2,1)S(1)} %reshape.371), channel_id=1, source_target_pairs={{0,16},{1,17},{2,18},{3,19},{4,20},{5,21},{6,22},{7,23},{8,24},{9,... | collective-permute-start | bytes 1736 | tf_op jit(solution)/shard_map/ppermute | solution.py:144
  6.3 28.0 %collective-permute-start.10 = (bf16[24,768]{1,0:T(8,128)(2,1)S(1)}, bf16[24,768]{1,0:T(8,128)(2,1)S(1)}, u32[]{:S(2)}, u32[]{:S(2)}) collective-permute-start(bf16[24,768]{1,0:T(8,128)(2,1)S(1)} %convert_element_type.348), channel_id=1, source_target_pairs={{0,16},{1,17},{2,18},{3,19},{4,20},{5,21},{6,22},{7,23},{8,24},{9,... | collective-permute-start | bytes 110600 | tf_op jit(solution)/shard_map/ppermute | solution.py:144
  7.2 33.4 %collective-permute-start.5 = (bf16[24,2304]{1,0:T(8,128)(2,1)S(1)}, bf16[24,2304]{1,0:T(8,128)(2,1)S(1)}, u32[]{:S(2)}, u32[]{:S(2)}) collective-permute-start(bf16[24,2304]{1,0:T(8,128)(2,1)S(1)} %convert_element_type.336), channel_id=1, source_target_pairs={{0,16},{1,17},{2,18},{3,19},{4,20},{5,21},{6,22},{7,23},{8,24},{9,... | collective-permute-start | bytes 331784 | tf_op jit(solution)/shard_map/ppermute | solution.py:144
  11.2 31.0 %collective-permute-start.20 = (bf16[96,768]{1,0:T(8,128)(2,1)S(1)}, bf16[96,768]{1,0:T(8,128)(2,1)}, u32[]{:S(2)}, u32[]{:S(2)}) collective-permute-start(bf16[96,768]{1,0:T(8,128)(2,1)S(1)} %convert_element_type.352), channel_id=1, source_target_pairs={{0,16},{1,17},{2,18},{3,19},{4,20},{5,21},{6,22},{7,23},{8,24},{9,... | collective-permute-start | bytes 442376 | tf_op jit(solution)/shard_map/ppermute | solution.py:144
  12.3 32.5 %collective-permute-start.15 = (bf16[24,3072]{1,0:T(8,128)(2,1)S(1)}, bf16[24,3072]{1,0:T(8,128)(2,1)}, u32[]{:S(2)}, u32[]{:S(2)}) collective-permute-start(bf16[24,3072]{1,0:T(8,128)(2,1)S(1)} %convert_element_type.350), channel_id=1, source_target_pairs={{0,16},{1,17},{2,18},{3,19},{4,20},{5,21},{6,22},{7,23},{8,24},{9,... | collective-permute-start | bytes 442376 | tf_op jit(solution)/shard_map/ppermute | solution.py:144
  43.2 10.0 %collective-permute-start.21 = (bf16[2,96,768]{2,1,0:T(8,128)(2,1)S(1)}, bf16[2,96,768]{2,1,0:T(8,128)(2,1)S(1)}, u32[]{:S(2)}, u32[]{:S(2)}) collective-permute-start(bf16[2,96,768]{2,1,0:T(8,128)(2,1)S(1)} %pad_maximum_fusion.19), channel_id=1, source_target_pairs={{0,4},{1,5},{2,6},{3,7},{4,0},{5,1},{6,2},{7,3},{8,12},{9,13},{10,... | collective-permute-start | bytes 884744 | tf_op jit(solution)/shard_map/ppermute | solution.py:144
  46.5 13.0 %collective-permute-start.13 = (bf16[2,2,2,24,768]{4,3,2,1,0:T(8,128)(2,1)S(1)}, bf16[2,2,2,24,768]{4,3,2,1,0:T(8,128)(2,1)S(1)}, u32[]{:S(2)}, u32[]{:S(2)}) collective-permute-start(bf16[2,2,2,24,768]{4,3,2,1,0:T(8,128)(2,1)S(1)} %pad_maximum_fusion.17), channel_id=1, source_target_pairs={{0,4},{1,5},{2,6},{3,7},{4,0},{5,1},{6,2},{7,3},{8,12},{9,13},{10,... | collective-permute-start | bytes 884744 | tf_op jit(solution)/shard_map/ppermute | solution.py:144
  47.8 19.3 %collective-permute-start.7 = (bf16[2,2,24,2304]{3,2,1,0:T(8,128)(2,1)S(1)}, bf16[2,2,24,2304]{3,2,1,0:T(8,128)(2,1)S(1)}, u32[]{:S(2)}, u32[]{:S(2)}) collective-permute-start(bf16[2,2,24,2304]{3,2,1,0:T(8,128)(2,1)S(1)} %pad_maximum_fusion.16), channel_id=1, source_target_pairs={{0,4},{1,5},{2,6},{3,7},{4,0},{5,1},{6,2},{7,3},{8,12},{9,13},{10,... | collective-permute-start | bytes 1327112 | tf_op jit(solution)/shard_map/ppermute | solution.py:144
  53.3 16.3 %collective-permute-start.22 = (bf16[2,2,96,768]{3,2,1,0:T(8,128)(2,1)S(1)}, bf16[2,2,96,768]{3,2,1,0:T(8,128)(2,1)S(1)}, u32[]{:S(2)}, u32[]{:S(2)}) collective-permute-start(bf16[2,2,96,768]{3,2,1,0:T(8,128)(2,1)S(1)} %pad_maximum_fusion.15), channel_id=1, source_target_pairs={{0,2},{1,3},{2,0},{3,1},{4,6},{5,7},{6,4},{7,5},{8,10},{9,11},{10,... | collective-permute-start | bytes 1769480 | tf_op jit(solution)/shard_map/ppermute | solution.py:144
  54.0 28.3 %collective-permute-start.17 = (bf16[2,2,24,3072]{3,2,1,0:T(8,128)(2,1)S(1)}, bf16[2,2,24,3072]{3,2,1,0:T(8,128)(2,1)S(1)}, u32[]{:S(2)}, u32[]{:S(2)}) collective-permute-start(bf16[2,2,24,3072]{3,2,1,0:T(8,128)(2,1)S(1)} %pad_maximum_fusion.14), channel_id=1, source_target_pairs={{0,2},{1,3},{2,0},{3,1},{4,6},{5,7},{6,4},{7,5},{8,10},{9,11},{10,... | collective-permute-start | bytes 1769480 | tf_op jit(solution)/shard_map/ppermute | solution.py:144
  59.6 24.4 %collective-permute-start.14 = (bf16[2,2,2,2,24,768]{5,4,3,2,1,0:T(8,128)(2,1)S(1)}, bf16[2,2,2,2,24,768]{5,4,3,2,1,0:T(8,128)(2,1)S(1)}, u32[]{:S(2)}, u32[]{:S(2)}) collective-permute-start(bf16[2,2,2,2,24,768]{5,4,3,2,1,0:T(8,128)(2,1)S(1)} %pad_maximum_fusion.13), channel_id=1, source_target_pairs={{0,1},{1,0},{2,3},{3,2},{4,5},{5,4},{6,7},{7,6},{8,9},{9,8},{10,11... | collective-permute-start | bytes 1769480 | tf_op jit(solution)/shard_map/ppermute | solution.py:144
  67.2 29.2 %collective-permute-start.8 = (bf16[2,2,2,24,2304]{4,3,2,1,0:T(8,128)(2,1)S(1)}, bf16[2,2,2,24,2304]{4,3,2,1,0:T(8,128)(2,1)S(1)}, u32[]{:S(2)}, u32[]{:S(2)}) collective-permute-start(bf16[2,2,2,24,2304]{4,3,2,1,0:T(8,128)(2,1)S(1)} %pad_maximum_fusion.12), channel_id=1, source_target_pairs={{0,2},{1,3},{2,0},{3,1},{4,6},{5,7},{6,4},{7,5},{8,10},{9,11},{10,... | collective-permute-start | bytes 2654216 | tf_op jit(solution)/shard_map/ppermute | solution.py:144
  69.8 28.2 %collective-permute-start.23 = (bf16[2,2,2,96,768]{4,3,2,1,0:T(8,128)(2,1)S(1)}, bf16[2,2,2,96,768]{4,3,2,1,0:T(8,128)(2,1)S(1)}, u32[]{:S(2)}, u32[]{:S(2)}) collective-permute-start(bf16[2,2,2,96,768]{4,3,2,1,0:T(8,128)(2,1)S(1)} %pad_maximum_fusion.9), channel_id=1, source_target_pairs={{0,8},{1,9},{2,10},{3,11},{4,12},{5,13},{6,14},{7,15},{8,0},{9,1},... | collective-permute-start | bytes 3538952 | tf_op jit(solution)/shard_map/ppermute | solution.py:144
  82.5 18.5 %collective-permute-start.18 = (bf16[2,2,2,24,3072]{4,3,2,1,0:T(8,128)(2,1)S(1)}, bf16[2,2,2,24,3072]{4,3,2,1,0:T(8,128)(2,1)S(1)}, u32[]{:S(2)}, u32[]{:S(2)}) collective-permute-start(bf16[2,2,2,24,3072]{4,3,2,1,0:T(8,128)(2,1)S(1)} %pad_maximum_fusion.8), channel_id=1, source_target_pairs={{0,4},{1,5},{2,6},{3,7},{4,0},{5,1},{6,2},{7,3},{8,12},{9,13},{10,... | collective-permute-start | bytes 3538952 | tf_op jit(solution)/shard_map/ppermute | solution.py:144
  100.0 49.6 %collective-permute-start.24 = (bf16[2,2,2,2,96,768]{5,4,3,2,1,0:T(8,128)(2,1)}, bf16[2,2,2,2,96,768]{5,4,3,2,1,0:T(8,128)(2,1)}, u32[]{:S(2)}, u32[]{:S(2)}) collective-permute-start(bf16[2,2,2,2,96,768]{5,4,3,2,1,0:T(8,128)(2,1)} %pad_maximum_fusion.4), channel_id=1, source_target_pairs={{0,1},{1,0},{2,3},{3,2},{4,5},{5,4},{6,7},{7,6},{8,9},{9,8},{10,11... | collective-permute-start | bytes 7077896 | tf_op jit(solution)/shard_map/ppermute | solution.py:144
  103.9 52.5 %collective-permute-start.19 = (bf16[2,2,2,2,24,3072]{5,4,3,2,1,0:T(8,128)(2,1)}, bf16[2,2,2,2,24,3072]{5,4,3,2,1,0:T(8,128)(2,1)}, u32[]{:S(2)}, u32[]{:S(2)}) collective-permute-start(bf16[2,2,2,2,24,3072]{5,4,3,2,1,0:T(8,128)(2,1)} %pad_maximum_fusion.3), channel_id=1, source_target_pairs={{0,1},{1,0},{2,3},{3,2},{4,5},{5,4},{6,7},{7,6},{8,9},{9,8},{10,11... | collective-permute-start | bytes 7077896 | tf_op jit(solution)/shard_map/ppermute | solution.py:144
  366.8 17.0 %collective-permute-start.25 = (bf16[2,2,2,2,24,1152]{5,4,0,1,2,3:T(8,128)(2,1)}, bf16[2,2,2,2,24,1152]{5,4,0,1,2,3:T(8,128)(2,1)}, u32[]{:S(2)}, u32[]{:S(2)}) collective-permute-start(bf16[2,2,2,2,24,1152]{5,4,0,1,2,3:T(8,128)(2,1)} %fusion.50), channel_id=1, source_target_pairs={{0,1},{1,0},{2,3},{3,2},{4,5},{5,4},{6,7},{7,6},{8,9},{9,8},{10,11... | collective-permute-start | bytes 2654216 | tf_op jit(solution)/shard_map/ppermute | solution.py:176
  375.5 37.1 %collective-permute-start.45 = (bf16[2,2,2,2,96,768]{5,4,0,2,3,1:T(8,128)(2,1)}, bf16[2,2,2,2,96,768]{5,4,0,2,3,1:T(8,128)(2,1)S(1)}, u32[]{:S(2)}, u32[]{:S(2)}) collective-permute-start(bf16[2,2,2,2,96,768]{5,4,0,2,3,1:T(8,128)(2,1)} %fusion.34), channel_id=1, source_target_pairs={{0,1},{1,0},{2,3},{3,2},{4,5},{5,4},{6,7},{7,6},{8,9},{9,8},{10,11... | collective-permute-start | bytes 7077896 | tf_op jit(solution)/shard_map/ppermute | solution.py:176
  375.5 41.5 %collective-permute-start.40 = (bf16[2,2,2,2,24,3072]{5,4,0,1,3,2:T(8,128)(2,1)}, bf16[2,2,2,2,24,3072]{5,4,0,1,3,2:T(8,128)(2,1)S(1)}, u32[]{:S(2)}, u32[]{:S(2)}) collective-permute-start(bf16[2,2,2,2,24,3072]{5,4,0,1,3,2:T(8,128)(2,1)} %fusion.35), channel_id=1, source_target_pairs={{0,1},{1,0},{2,3},{3,2},{4,5},{5,4},{6,7},{7,6},{8,9},{9,8},{10,11... | collective-permute-start | bytes 7077896 | tf_op jit(solution)/shard_map/ppermute | solution.py:176
  379.0 9.9 %collective-permute-start.30 = (bf16[2,2,2,2,24,1152]{5,4,0,1,3,2:T(8,128)(2,1)}, bf16[2,2,2,2,24,1152]{5,4,0,1,3,2:T(8,128)(2,1)S(1)}, u32[]{:S(2)}, u32[]{:S(2)}) collective-permute-start(bf16[2,2,2,2,24,1152]{5,4,0,1,3,2:T(8,128)(2,1)} %fusion.51), channel_id=1, source_target_pairs={{0,1},{1,0},{2,3},{3,2},{4,5},{5,4},{6,7},{7,6},{8,9},{9,8},{10,11... | collective-permute-start | bytes 2654216 | tf_op jit(solution)/shard_map/ppermute | solution.py:176
  385.2 12.3 %collective-permute-start.26 = (bf16[2,2,2,24,1152]{4,3,0,1,2:T(8,128)(2,1)S(1)}, bf16[2,2,2,24,1152]{4,3,0,1,2:T(8,128)(2,1)S(1)}, u32[]{:S(2)}, u32[]{:S(2)}) collective-permute-start(bf16[2,2,2,24,1152]{4,3,0,1,2:T(8,128)(2,1)S(1)} %fusion.56), channel_id=1, source_target_pairs={{0,2},{1,3},{2,0},{3,1},{4,6},{5,7},{6,4},{7,5},{8,10},{9,11},{10,... | collective-permute-start | bytes 1327112 | tf_op jit(solution)/shard_map/ppermute | solution.py:176
  392.9 12.5 %collective-permute-start.31 = (bf16[2,2,2,24,1152]{4,3,0,1,2:T(8,128)(2,1)S(1)}, bf16[2,2,2,24,1152]{4,3,0,1,2:T(8,128)(2,1)S(1)}, u32[]{:S(2)}, u32[]{:S(2)}) collective-permute-start(bf16[2,2,2,24,1152]{4,3,0,1,2:T(8,128)(2,1)S(1)} %fusion.57), channel_id=1, source_target_pairs={{0,4},{1,5},{2,6},{3,7},{4,0},{5,1},{6,2},{7,3},{8,12},{9,13},{10,... | collective-permute-start | bytes 1327112 | tf_op jit(solution)/shard_map/ppermute | solution.py:176
  397.7 10.0 %collective-permute-start.27 = (bf16[2,2,24,1152]{3,2,0,1:T(8,128)(2,1)S(1)}, bf16[2,2,24,1152]{3,2,0,1:T(8,128)(2,1)S(1)}, u32[]{:S(2)}, u32[]{:S(2)}) collective-permute-start(bf16[2,2,24,1152]{3,2,0,1:T(8,128)(2,1)S(1)} %fusion.64), channel_id=1, source_target_pairs={{0,4},{1,5},{2,6},{3,7},{4,0},{5,1},{6,2},{7,3},{8,12},{9,13},{10,... | collective-permute-start | bytes 663560 | tf_op jit(solution)/shard_map/ppermute | solution.py:176
  411.6 10.2 %collective-permute-start.33 = (bf16[2,24,1152]{2,1,0:T(8,128)(2,1)S(1)}, bf16[2,24,1152]{2,1,0:T(8,128)(2,1)S(1)}, u32[]{:S(2)}, u32[]{:S(2)}) collective-permute-start(bf16[2,24,1152]{2,1,0:T(8,128)(2,1)S(1)} %fusion.70), channel_id=1, source_target_pairs={{0,8},{1,9},{2,10},{3,11},{4,12},{5,13},{6,14},{7,15},{8,0},{9,1},... | collective-permute-start | bytes 331784 | tf_op jit(solution)/shard_map/ppermute | solution.py:176
  415.9 27.4 %collective-permute-start.46 = (bf16[2,2,2,96,768]{4,3,0,1,2:T(8,128)(2,1)S(1)}, bf16[2,2,2,96,768]{4,3,0,1,2:T(8,128)(2,1)S(1)}, u32[]{:S(2)}, u32[]{:S(2)}) collective-permute-start(bf16[2,2,2,96,768]{4,3,0,1,2:T(8,128)(2,1)S(1)} %fusion.46), channel_id=1, source_target_pairs={{0,8},{1,9},{2,10},{3,11},{4,12},{5,13},{6,14},{7,15},{8,0},{9,1},... | collective-permute-start | bytes 3538952 | tf_op jit(solution)/shard_map/ppermute | solution.py:176
  418.2 26.9 %collective-permute-start.41 = (bf16[2,2,2,24,3072]{4,3,0,1,2:T(8,128)(2,1)S(1)}, bf16[2,2,2,24,3072]{4,3,0,1,2:T(8,128)(2,1)S(1)}, u32[]{:S(2)}, u32[]{:S(2)}) collective-permute-start(bf16[2,2,2,24,3072]{4,3,0,1,2:T(8,128)(2,1)S(1)} %fusion.45), channel_id=1, source_target_pairs={{0,4},{1,5},{2,6},{3,7},{4,0},{5,1},{6,2},{7,3},{8,12},{9,13},{10,... | collective-permute-start | bytes 3538952 | tf_op jit(solution)/shard_map/ppermute | solution.py:176
  419.2 27.0 %collective-permute-start.29 = (bf16[24,1152]{1,0:T(8,128)(2,1)S(1)}, bf16[24,1152]{1,0:T(8,128)(2,1)S(1)}, u32[]{:S(2)}, u32[]{:S(2)}) collective-permute-start(bf16[24,1152]{1,0:T(8,128)(2,1)S(1)} %fusion.73), channel_id=1, source_target_pairs={{0,16},{1,17},{2,18},{3,19},{4,20},{5,21},{6,22},{7,23},{8,24},{9,... | collective-permute-start | bytes 165896 | tf_op jit(solution)/shard_map/ppermute | solution.py:176
  421.8 58.2 %collective-permute-start.34 = (bf16[24,1152]{1,0:T(8,128)(2,1)S(1)}, bf16[24,1152]{1,0:T(8,128)(2,1)S(1)}, u32[]{:S(2)}, u32[]{:S(2)}) collective-permute-start(bf16[24,1152]{1,0:T(8,128)(2,1)S(1)} %fusion.74), channel_id=1, source_target_pairs={{0,16},{1,17},{2,18},{3,19},{4,20},{5,21},{6,22},{7,23},{8,24},{9,... | collective-permute-start | bytes 165896 | tf_op jit(solution)/shard_map/ppermute | solution.py:176
  443.6 16.3 %collective-permute-start.47 = (bf16[2,2,96,768]{3,2,0,1:T(8,128)(2,1)S(1)}, bf16[2,2,96,768]{3,2,0,1:T(8,128)(2,1)S(1)}, u32[]{:S(2)}, u32[]{:S(2)}) collective-permute-start(bf16[2,2,96,768]{3,2,0,1:T(8,128)(2,1)S(1)} %fusion.53), channel_id=1, source_target_pairs={{0,2},{1,3},{2,0},{3,1},{4,6},{5,7},{6,4},{7,5},{8,10},{9,11},{10,... | collective-permute-start | bytes 1769480 | tf_op jit(solution)/shard_map/ppermute | solution.py:176
  445.5 23.1 %collective-permute-start.42 = (bf16[2,2,24,3072]{3,2,0,1:T(8,128)(2,1)S(1)}, bf16[2,2,24,3072]{3,2,0,1:T(8,128)(2,1)S(1)}, u32[]{:S(2)}, u32[]{:S(2)}) collective-permute-start(bf16[2,2,24,3072]{3,2,0,1:T(8,128)(2,1)S(1)} %fusion.52), channel_id=1, source_target_pairs={{0,2},{1,3},{2,0},{3,1},{4,6},{5,7},{6,4},{7,5},{8,10},{9,11},{10,... | collective-permute-start | bytes 1769480 | tf_op jit(solution)/shard_map/ppermute | solution.py:176
  469.6 19.7 %collective-permute-start.49 = (bf16[96,768]{1,0:T(8,128)(2,1)}, bf16[96,768]{1,0:T(8,128)(2,1)S(1)}, u32[]{:S(2)}, u32[]{:S(2)}) collective-permute-start(bf16[96,768]{1,0:T(8,128)(2,1)} %fusion.68), channel_id=1, source_target_pairs={{0,16},{1,17},{2,18},{3,19},{4,20},{5,21},{6,22},{7,23},{8,24},{9,... | collective-permute-start | bytes 442376 | tf_op jit(solution)/shard_map/ppermute | solution.py:176
  505.0 17.6 %collective-permute-start.59 = (f32[8,128]{1,0:T(8,128)}, f32[8,128]{1,0:T(8,128)}, u32[]{:S(2)}, u32[]{:S(2)}) collective-permute-start(f32[8,128]{1,0:T(8,128)} %add.474), channel_id=1, source_target_pairs={{0,16},{1,17},{2,18},{3,19},{4,20},{5,21},{6,22},{7,23},{8,24},{9,... | collective-permute-start | bytes 12296 | tf_op jit(solution)/shard_map/ppermute | solution.py:185
  (123 other events, 1594.2 us)
